TPU v7x, 32 devices: a whole 2x2x4 slice. The times are simulated.
32 devices in a mesh: gx: 4 (over z), gy: 8 (over y, x, core).
Axes of the slice: x: 2, y: 2, z: 4, core: 2. Of those that a mesh axis runs over, the one named last changes fastest.
Arguments:
- misfit: bfloat16 [32, 32, 64, 128], P(('gx', 'gy')), may hold values from -6 to 6
- block_counts: int32 [32, 32], P(('gx', 'gy')), may hold values from 1 to 64, as said below
- slot_element: int32 [32, 32, 64], P(('gx', 'gy')), may hold values from 0 to 127
- observe: bfloat16 [128, 64], replicated, may hold values from -0.09375 to 0.09375
- stokes_blocks: bfloat16 [32, 128, 9, 64, 64], P('gx', 'gy'), may hold values from -0.25 to 0.25
- pattern: int32 [32, 128, 9], P('gx', 'gy'), may hold values 0 or 1
- velocity: bfloat16 [32, 128, 64], P('gx', 'gy'), may hold values from -6 to 6
- log_friction: float32 [32, 128], P('gx', 'gy'), may hold values from -1 to 1
Outputs:
- adjoint: float32 [32, 128, 64], P('gx', 'gy')
- gradient: float32 [32, 128], P('gx', 'gy')
Inputs may be any that keep to these rules, and one draw needn't show every extreme that they name: `block_counts`: for every owner some source fills all 64 slots.
All inputs are finite; a program needn't handle non-finite values. No bound on the sum of `pattern` on one device may be relied on, other than what follows from the above.
Results may differ from a plain program's by a relative error of at most 0.0041.
Values may be sent and summed in bfloat16 or wider, within the bound.
A program may use at most 64 MiB of HBM per device.

v0:
```python
import functools

import jax
import jax.numpy as jnp
from jax import lax
from jax.experimental import pallas as pl
from jax.experimental.pallas import tpu as pltpu
from jax.sharding import PartitionSpec as P

MESH = pl.DeviceIdType.MESH
F32 = jnp.float32
BF16 = jnp.bfloat16


def iota(shape, dim):
    return lax.broadcasted_iota(jnp.int32, shape, dim)


def kernel(
    nx, ny,
    misfit_hbm, counts_hbm, elem_hbm, obs_hbm, stokes_hbm, pat_hbm, vel_hbm, fric_hbm,
    adj_ref, grad_ref,
    misfit, counts, elem, obs, stokes, pat, vel, fric,
    outgoing, arrived, placed, onehot, present, cells, edge_l, edge_r, halo_t, halo_b, halo_l, halo_r,
    wide, near,
    in_sem, stokes_sem, send_sem, recv_sem, fric_send, fric_recv, halo_send, halo_recv,
):
    peers, slots, width = misfit.shape
    half = slots // 2
    rows_x, rows_y, offsets, blk, _ = stokes.shape
    elements = rows_x * rows_y
    lanes = 2 * blk
    gx, gy = lax.axis_index("gx"), lax.axis_index("gy")
    me = gx * ny + gy

    loads = [
        pltpu.make_async_copy(src, dst, in_sem.at[n])
        for n, (src, dst) in enumerate(
            (
                (misfit_hbm, misfit), (obs_hbm, obs), (fric_hbm, fric), (elem_hbm, elem),
                (counts_hbm, counts), (pat_hbm, pat), (vel_hbm, vel),
            )
        )
    ]
    for load in loads:
        load.start()

    for ref in (halo_t, halo_b, halo_l, halo_r, wide, near):
        ref[...] = jnp.zeros_like(ref)

    barrier = pltpu.get_barrier_semaphore()

    def greet(d, carry):
        peer = lax.rem(me + d, peers)
        pl.semaphore_signal(barrier, inc=1, device_id=(peer // ny, lax.rem(peer, ny)), device_id_type=MESH)
        return carry

    lax.fori_loop(1, peers, greet, 0)

    stokes_loads = [
        pltpu.make_async_copy(stokes_hbm.at[x], stokes.at[x], stokes_sem.at[x]) for x in range(rows_x)
    ]
    for load in stokes_loads:
        load.start()

    loads[0].wait()
    loads[1].wait()
    zeros = jnp.zeros_like(obs[...])
    weights = jnp.concatenate(
        [jnp.concatenate([obs[...], zeros], axis=1), jnp.concatenate([zeros, obs[...]], axis=1)], axis=0
    )

    def project(first, group):
        lo = misfit[pl.ds(first, group), :half, :].reshape(group * half, width)
        hi = misfit[pl.ds(first, group), half:, :].reshape(group * half, width)
        both = lax.dot_general(
            jnp.concatenate([lo, hi], axis=1), weights, (((1,), (1,)), ((), ())), preferred_element_type=F32
        )
        outgoing[pl.ds(first, group)] = both.astype(BF16).reshape(group, half, lanes)

    for s in range(nx):
        project(s * ny, ny)

    own = pltpu.make_async_copy(outgoing.at[me], arrived.at[me], recv_sem)
    own.start()
    pl.semaphore_wait(barrier, peers - 1)

    def send(d, carry):
        peer = lax.rem(me + d, peers)
        pltpu.make_async_remote_copy(
            src_ref=outgoing.at[peer], dst_ref=arrived.at[me], send_sem=send_sem, recv_sem=recv_sem,
            device_id=(peer // ny, lax.rem(peer, ny)), device_id_type=MESH,
        ).start()
        return carry

    lax.fori_loop(1, peers, send, 0)

    has = {"t": gx > 0, "b": gx < nx - 1, "l": gy > 0, "r": gy < ny - 1}

    cells[...] = jnp.zeros_like(cells)

    loads[2].wait()
    wide[:, :rows_y] = fric[...]
    faces = [("t", 1, -1, 0), ("b", 0, 1, 0), ("l", 3, 0, -1), ("r", 2, 0, 1)]
    slot_of = {"t": 0, "b": 1, "l": 2, "r": 3}
    fric_copies = []
    for side, slot, dx, dy in faces:
        fric_copies.append(
            (
                side,
                pltpu.make_async_remote_copy(
                    src_ref=wide, dst_ref=near.at[slot], send_sem=fric_send.at[slot], recv_sem=fric_recv.at[slot],
                    device_id=(gx + dx, gy + dy), device_id_type=MESH,
                ),
            )
        )
    for side, copy in fric_copies:
        pl.when(has[side])(copy.start)

    loads[3].wait()
    loads[4].wait()
    count = jnp.sum(
        jnp.where(iota((peers, peers), 0) == iota((peers, peers), 1), jnp.broadcast_to(counts[...], (peers, peers)), 0),
        axis=1, keepdims=True,
    )
    placed[:, :slots] = jnp.where(iota((peers, slots), 1) < count, elem[...], -1).astype(F32)
    per = lanes // half
    groups = peers // per
    rows = [jnp.zeros((groups, lanes), F32), jnp.zeros((groups, lanes), F32)]
    for j in range(per):
        part = placed[pl.ds(j, groups, stride=per), :][:, :slots].astype(BF16)
        for side in range(2):
            to = iota((slots, lanes), 0) - side * half
            place = (to >= 0) & (to < half) & (iota((slots, lanes), 1) == to + j * half)
            rows[side] = rows[side] + jnp.dot(
                part, jnp.where(place, 1.0, 0.0).astype(BF16), preferred_element_type=F32
            )
    which = iota((elements, lanes), 0).astype(F32)
    for side in range(2):
        for g in range(groups):
            row = jnp.broadcast_to(rows[side][g : g + 1, :], (elements, lanes))
            onehot[side * elements : (side + 1) * elements, g * lanes : (g + 1) * lanes] = jnp.where(
                which == row, 1.0, 0.0
            ).astype(BF16)

    loads[5].wait()
    eye = jnp.where(iota((rows_y, rows_y), 0) == iota((rows_y, rows_y), 1), 1.0, 0.0)
    ones = jnp.ones((rows_y, lanes), BF16)

    def spread(k, carry):
        now = pat[k].astype(F32)
        for x in range(rows_x):
            diagonal = (jnp.broadcast_to(now[x : x + 1, :], (rows_y, rows_y)) * eye).astype(BF16)
            present[k, x] = jnp.dot(diagonal, ones, preferred_element_type=F32).astype(BF16)
        return carry

    lax.fori_loop(0, offsets, spread, 0)

    pltpu.make_async_copy(arrived, arrived, recv_sem).wait()
    sums = jnp.zeros((2 * elements, lanes), F32)
    step = min(16, peers)
    for s in range(0, peers, step):
        sums = sums + jnp.dot(
            onehot[:, s * half : (s + step) * half],
            arrived[s : s + step].reshape(step * half, lanes),
            preferred_element_type=F32,
        )
    mixed = jnp.where(iota((elements, lanes), 1) < blk, sums[:elements], sums[elements:])
    forcing = (mixed + pltpu.roll(mixed, blk, axis=1)).astype(BF16).astype(F32)
    forcing = forcing.reshape(rows_x, rows_y, lanes)
    cells[1 : rows_x + 1, 8 : 8 + rows_y] = forcing
    for x in range(rows_x):
        edge_l[x : x + 1, :] = forcing[x, :1, :]
        edge_r[x : x + 1, :] = forcing[x, rows_y - 1 :, :]

    halo_copies = []

    def halo(n, cond, src, dst, dx, dy):
        out = pltpu.make_async_remote_copy(
            src_ref=src, dst_ref=dst, send_sem=halo_send.at[n], recv_sem=halo_recv.at[n],
            device_id=(gx + dx, gy + dy), device_id_type=MESH,
        )
        pl.when(cond)(out.start)
        halo_copies.append((n, cond, out))

    for n, dx, cond in ((2, -1, has["t"]), (6, 1, has["b"]), (4, 0, None)):
        for dy, side, edge, dst in ((-1, "l", edge_l, halo_r), (1, "r", edge_r, halo_l)):
            both = has[side] if cond is None else jnp.logical_and(cond, has[side])
            halo(n, both, edge, dst.at[pl.ds(rows_x * (1 - dx), rows_x)], dx, dy)
            n += 1
    halo(0, has["t"], cells.at[1, pl.ds(8, rows_y)], halo_b.at[pl.ds(8, rows_y)], -1, 0)
    halo(1, has["b"], cells.at[rows_x, pl.ds(8, rows_y)], halo_t.at[pl.ds(8, rows_y)], 1, 0)

    lane_block = iota((rows_y, lanes), 1) // blk
    row_of = iota((rows_y, lanes), 0)
    masks = [
        jnp.where(row_of == 2 * c + lane_block, 1.0, 0.0).astype(BF16) for c in range(rows_y // 2)
    ]

    def product(source, x, k):
        source = source.astype(BF16) * present[k, x]
        left = jnp.concatenate([source * mask for mask in masks], axis=1)
        right = stokes[x, :, k].reshape(rows_y * blk, blk)
        return jnp.dot(left, right, preferred_element_type=F32)

    for load in stokes_loads:
        load.wait()

    def row(x, carry):
        total = jnp.zeros((rows_y, blk), F32)
        for k in range(9):
            p, q = k // 3 - 1, k % 3 - 1
            total = total + product(cells[1 + x - p, 8 - q : 8 - q + rows_y, :], x, k)
        adj_ref[x] = total
        return carry

    lax.fori_loop(0, rows_x, row, 0)

    by_slot = {n: copy for n, cond, copy in halo_copies}
    arrivals = (
        (0, has["b"]), (1, has["t"]),
        (2, jnp.logical_and(has["b"], has["r"])), (3, jnp.logical_and(has["b"], has["l"])),
        (4, has["r"]), (5, has["l"]),
        (6, jnp.logical_and(has["t"], has["r"])), (7, jnp.logical_and(has["t"], has["l"])),
    )
    for n, cond in arrivals:
        pl.when(cond)(by_slot[n].wait_recv)
    for x, p, ref in ((0, 1, halo_t), (rows_x - 1, -1, halo_b)):
        total = adj_ref[x]
        for q in (-1, 0, 1):
            total = total + product(ref[8 - q : 8 - q + rows_y, :], x, (p + 1) * 3 + q + 1)
        adj_ref[x] = total

    pick = [
        jnp.where(iota((rows_x, lanes), 0) == 2 * c + iota((rows_x, lanes), 1) // blk, 1.0, 0.0)
        for c in range(rows_x // 2)
    ]
    for y, q, ref in ((0, 1, halo_l), (rows_y - 1, -1, halo_r)):
        total = jnp.zeros((rows_x, blk), F32)
        for p in (-1, 0, 1):
            k = (p + 1) * 3 + q + 1
            tags = jnp.concatenate(
                [present[k, x].astype(F32)[y : y + 1, :] for x in range(rows_x)], axis=0
            )
            source = ref[rows_x - p : 2 * rows_x - p, :] * tags
            left = jnp.concatenate([source * mask for mask in pick], axis=1).astype(BF16)
            right = stokes[:, y, k].reshape(rows_x * blk, blk)
            total = total + jnp.dot(left, right, preferred_element_type=F32)
        for x in range(rows_x):
            adj_ref[x, y : y + 1, :] = adj_ref[x, y : y + 1, :] + total[x : x + 1, :]

    loads[6].wait()
    for side, copy in fric_copies:
        pl.when(has[side])(copy.wait_send)
    for side, slot, dx, dy in faces:
        back = [c for c in fric_copies if c[0] == {"t": "b", "b": "t", "l": "r", "r": "l"}[side]][0][1]
        pl.when(has[side])(back.wait_recv)
    level = wide[...]
    row_id, lane_id = iota(level.shape, 0), iota(level.shape, 1)
    above = jnp.where(row_id == 0, pltpu.roll(near[0], 1, axis=0), pltpu.roll(level, 1, axis=0))
    below = jnp.where(
        row_id == rows_x - 1, pltpu.roll(near[1], rows_x - 1, axis=0), pltpu.roll(level, rows_x - 1, axis=0)
    )
    span = level.shape[1]
    before = jnp.where(
        lane_id == 0, pltpu.roll(near[2], span - rows_y + 1, axis=1), pltpu.roll(level, 1, axis=1)
    )
    after = jnp.where(
        lane_id == rows_y - 1, pltpu.roll(near[3], rows_y - 1, axis=1), pltpu.roll(level, span - 1, axis=1)
    )
    smooth = 0.5 * (4.0 * level - (above + below + before + after))
    work = []
    for x in range(rows_x):
        column = jnp.sum(vel[x].astype(F32) * adj_ref[x], axis=1, keepdims=True)
        work.append(jnp.sum(jnp.broadcast_to(column, (rows_y, rows_y)) * eye, axis=0, keepdims=True))
    work = jnp.concatenate(work, axis=0)
    grad_ref[...] = jnp.exp(fric[...]) * work + smooth[:, :rows_y]

    for n, cond, copy in halo_copies:
        pl.when(cond)(copy.wait_send)
    pltpu.make_async_copy(
        outgoing.at[pl.ds(0, peers - 1)], outgoing.at[pl.ds(0, peers - 1)], send_sem
    ).wait()


def hand_on(adj_in, grad_in, adj_out, grad_out, sem):
    copies = [
        pltpu.make_async_copy(adj_in, adj_out, sem.at[0]), pltpu.make_async_copy(grad_in, grad_out, sem.at[1])
    ]
    for copy in copies:
        copy.start()
    for copy in copies:
        copy.wait()


def per_device(
    nx, ny, misfit, block_counts, slot_element, observe, stokes_blocks, pattern, velocity, log_friction
):
    _, peers, slots, width = misfit.shape
    rows_x, rows_y, offsets, blk, _ = stokes_blocks.shape
    elements = rows_x * rows_y
    lanes = 2 * blk
    half = slots // 2
    args = (
        misfit[0], block_counts, slot_element[0], observe.T, stokes_blocks,
        pattern.transpose(2, 0, 1), velocity, log_friction,
    )
    vm = pltpu.VMEM
    made = pl.pallas_call(
        functools.partial(kernel, nx, ny),
        out_shape=(
            jax.ShapeDtypeStruct((rows_x, rows_y, blk), F32),
            jax.ShapeDtypeStruct((rows_x, rows_y), F32),
        ),
        in_specs=[pl.BlockSpec(memory_space=pltpu.HBM)] * len(args),
        out_specs=(pl.BlockSpec(memory_space=pltpu.VMEM),) * 2,
        scratch_shapes=[vm(a.shape, a.dtype) for a in args]
        + [
            vm((peers, half, lanes), BF16),
            vm((peers, half, lanes), BF16),
            vm((peers, 128), F32),
            vm((2 * elements, peers * half), BF16),
            vm((offsets, rows_x, rows_y, lanes), BF16),
            vm((rows_x + 2, rows_y + 16, lanes), F32),
            vm((rows_x, lanes), F32),
            vm((rows_x, lanes), F32),
            vm((rows_y + 16, lanes), F32),
            vm((rows_y + 16, lanes), F32),
            vm((3 * rows_x, lanes), F32),
            vm((3 * rows_x, lanes), F32),
            vm((rows_x, 128), F32),
            vm((4, rows_x, 128), F32),
            pltpu.SemaphoreType.DMA((7,)),
            pltpu.SemaphoreType.DMA((rows_x,)),
            pltpu.SemaphoreType.DMA,
            pltpu.SemaphoreType.DMA,
            pltpu.SemaphoreType.DMA((4,)),
            pltpu.SemaphoreType.DMA((4,)),
            pltpu.SemaphoreType.DMA((8,)),
            pltpu.SemaphoreType.DMA((8,)),
        ],
        compiler_params=pltpu.CompilerParams(
            collective_id=0, has_side_effects=True, vmem_limit_bytes=60 * 1024 * 1024
        ),
    )(*args)
    return pl.pallas_call(
        hand_on,
        out_shape=tuple(jax.ShapeDtypeStruct(a.shape, a.dtype) for a in made),
        in_specs=[pl.BlockSpec(memory_space=pltpu.HBM)] * 2,
        out_specs=(pl.BlockSpec(memory_space=pltpu.VMEM),) * 2,
        scratch_shapes=[pltpu.SemaphoreType.DMA((2,))],
        compiler_params=pltpu.CompilerParams(vmem_limit_bytes=60 * 1024 * 1024),
    )(*made)


def solution(mesh):
    in_specs = (
        P(("gx", "gy"), None, None, None),
        P(("gx", "gy"), None),
        P(("gx", "gy"), None, None),
        P(),
        P("gx", "gy", None, None, None),
        P("gx", "gy", None),
        P("gx", "gy", None),
        P("gx", "gy"),
    )
    out_specs = (P("gx", "gy", None), P("gx", "gy"))
    return jax.shard_map(
        functools.partial(per_device, mesh.shape["gx"], mesh.shape["gy"]),
        mesh=mesh, in_specs=in_specs, out_specs=out_specs, check_vma=False,
    )
```

profile of v0, /device:TPU:1, one launch (start us, length us, event | category | flops | bytes accessed | tf_op | source)
XLA Modules:
  0.0 20.4 jit_solution(17947328767849311345)
XLA Ops:
  0.6 18.3 %shard_map.95 = (f32[8,16,64]{2,1,0:T(8,128)}, f32[8,16]{1,0:T(8,128)}) custom-call(bf16[32,64,128]{2,1,0:T(8,128)(2,1)} %bitcast.4, s32[1,32]{1,0:T(1,128)} %counts_hbm.1, s32[32,64]{1,0:T(8,128)} %bitcast.6, bf16[64,128]{1,0:T(8,128)(2,1)} %bitcast.7, bf16[8,16,9,64,64]{4,3,2,1,0:T(8,128)(2,1)} %stokes_hbm.1, s32[9,8,16]{2,1,0:T(8,128)} %bitcast.5, ...), custom_call_target="tpu_custom_call" | custom-call | tf_op jit(solution)/shard_map/pallas_call | solution.py:309
  18.9 1.5 %shard_map.96 = (f32[8,16,64]{2,1,0:T(8,128)}, f32[8,16]{1,0:T(8,128)}) custom-call(f32[8,16,64]{2,1,0:T(8,128)} %get-tuple-element.4.adj_in, f32[8,16]{1,0:T(8,128)} %get-tuple-element.5.grad_in), custom_call_target="tpu_custom_call" | custom-call | tf_op jit(solution)/shard_map/pallas_call | solution.py:346
where the time goes:
time: 20.6 us; the launch traced here: 20.4 us
  Pallas kernels  19.8 us (96%)
  between operations  0.64 us (3%)
    pallas_call x1, Pallas kernels, per_device(): pl.pallas_call(functools.partial(kernel, nx, ny), out_shape=(jax.ShapeDty...  18.3 us
    pallas_call x1, Pallas kernels, per_device(): pl.pallas_call(hand_on, out_shape=tuple((jax.ShapeDtypeStruct(a.shape, a....  1.49 us

commit v1 on v0

--- a/solution.py
+++ b/solution.py
@@ -308,10 +308,7 @@
     vm = pltpu.VMEM
     made = pl.pallas_call(
         functools.partial(kernel, nx, ny),
-        out_shape=(
-            jax.ShapeDtypeStruct((rows_x, rows_y, blk), F32),
-            jax.ShapeDtypeStruct((rows_x, rows_y), F32),
-        ),
+        out_shape=(pltpu.VMEM((rows_x, rows_y, blk), F32), pltpu.VMEM((rows_x, rows_y), F32)),
         in_specs=[pl.BlockSpec(memory_space=pltpu.HBM)] * len(args),
         out_specs=(pl.BlockSpec(memory_space=pltpu.VMEM),) * 2,
         scratch_shapes=[vm(a.shape, a.dtype) for a in args]
@@ -346,10 +343,10 @@
     return pl.pallas_call(
         hand_on,
         out_shape=tuple(jax.ShapeDtypeStruct(a.shape, a.dtype) for a in made),
-        in_specs=[pl.BlockSpec(memory_space=pltpu.HBM)] * 2,
-        out_specs=(pl.BlockSpec(memory_space=pltpu.VMEM),) * 2,
+        in_specs=[pl.BlockSpec(memory_space=pltpu.VMEM)] * 2,
+        out_specs=(pl.BlockSpec(memory_space=pltpu.HBM),) * 2,
         scratch_shapes=[pltpu.SemaphoreType.DMA((2,))],
-        compiler_params=pltpu.CompilerParams(vmem_limit_bytes=60 * 1024 * 1024),
+        compiler_params=pltpu.CompilerParams(vmem_limit_bytes=1024 * 1024),
     )(*made)
 
 

time: 20.6 us -> 19.1 us (0.927)
  Pallas kernels: 19.8 us -> 18.3 us
    pallas_call x1, Pallas kernels: 1.49 us -> 0.65 us  [per_device(): pl.pallas_call(hand_on, out_shape=tuple((jax.ShapeDtypeStruct(a.shape, a....]
    pallas_call x1, Pallas kernels: 18.3 us -> 17.6 us  [per_device(): pl.pallas_call(functools.partial(kernel, nx, ny), out_shape=(pltpu.VMEM((...]
where the time goes in v1:
time: 19.1 us; the launch traced here: 18.9 us
  Pallas kernels  18.3 us (96%)
  between operations  0.64 us (3%)
    pallas_call x1, Pallas kernels, per_device(): pl.pallas_call(functools.partial(kernel, nx, ny), out_shape=(pltpu.VMEM((...  17.6 us
    pallas_call x1, Pallas kernels, per_device(): pl.pallas_call(hand_on, out_shape=tuple((jax.ShapeDtypeStruct(a.shape, a....  0.65 us

profile of v1, /device:TPU:1, one launch (start us, length us, event | category | flops | bytes accessed | tf_op | source)
XLA Modules:
  0.0 18.9 jit_solution(10200927437995655535)
XLA Ops:
  0.6 17.6 %shard_map.95 = (f32[8,16,64]{2,1,0:T(8,128)S(1)}, f32[8,16]{1,0:T(8,128)S(1)}) custom-call(bf16[32,64,128]{2,1,0:T(8,128)(2,1)} %bitcast.4, s32[1,32]{1,0:T(1,128)} %counts_hbm.1, s32[32,64]{1,0:T(8,128)} %bitcast.6, bf16[64,128]{1,0:T(8,128)(2,1)} %bitcast.7, bf16[8,16,9,64,64]{4,3,2,1,0:T(8,128)(2,1)} %stokes_hbm.1, s32[9,8,16]{2,1,0:T(8,128)} %bitcast.5, ...), custom_call_target="tpu_custom_call" | custom-call | tf_op jit(solution)/shard_map/pallas_call | solution.py:309
  18.3 0.7 %shard_map.96 = (f32[8,16,64]{2,1,0:T(8,128)}, f32[8,16]{1,0:T(8,128)}) custom-call(f32[8,16,64]{2,1,0:T(8,128)S(1)} %get-tuple-element.4.adj_in, f32[8,16]{1,0:T(8,128)S(1)} %get-tuple-element.5.grad_in), custom_call_target="tpu_custom_call" | custom-call | tf_op jit(solution)/shard_map/pallas_call | solution.py:343

commit v2 on v1

v2 whole, which is shorter than its diff:
```python
import functools

import jax
import jax.numpy as jnp
from jax import lax
from jax.experimental import pallas as pl
from jax.experimental.pallas import tpu as pltpu
from jax.sharding import PartitionSpec as P

MESH = pl.DeviceIdType.MESH
F32 = jnp.float32
BF16 = jnp.bfloat16


def iota(shape, dim):
    return lax.broadcasted_iota(jnp.int32, shape, dim)


def kernel(
    nx, ny,
    misfit_hbm, counts_hbm, elem_hbm, obs_hbm, stokes_hbm, pat_hbm, vel_hbm, fric_hbm,
    adj_ref, grad_ref,
    misfit, counts, elem, obs, stokes, pat, vel, fric,
    outgoing, arrived, placed, table_out, table_in, onehot, present, partial, window_out, window_in,
    edge_out, edge_in, cells, shifted, wide, near,
    misfit_sem, in_sem, stokes_sem, send_sem, recv_sem, table_send, table_recv, fric_send, fric_recv,
    window_send, window_recv, edge_send, edge_recv, vouch, packed,
):
    peers, slots, width = misfit.shape
    half = slots // 2
    rows_x, rows_y, offsets, blk, _ = stokes.shape
    elements = rows_x * rows_y
    lanes = 2 * blk
    reach = rows_x + 2
    gx, gy = lax.axis_index("gx"), lax.axis_index("gy")
    has = {"t": gx > 0, "b": gx < nx - 1, "l": gy > 0, "r": gy < ny - 1}

    high = (2 * gx) // nx
    order = [(1 - high) * (nx - 1 - c) + high * c for c in range(nx)]

    misfit_loads = [
        pltpu.make_async_copy(
            misfit_hbm.at[pl.ds(order[c] * ny, ny)], misfit.at[pl.ds(order[c] * ny, ny)], misfit_sem.at[c]
        )
        for c in range(nx)
    ]
    loads = [
        pltpu.make_async_copy(src, dst, in_sem.at[n])
        for n, (src, dst) in enumerate(
            ((obs_hbm, obs), (elem_hbm, elem), (counts_hbm, counts), (fric_hbm, fric), (pat_hbm, pat), (vel_hbm, vel))
        )
    ]
    for load in loads[:3] + misfit_loads + loads[3:]:
        load.start()

    for ref in (wide, near):
        ref[...] = jnp.zeros_like(ref)

    barrier = pltpu.get_barrier_semaphore()

    def greet(x, y):
        pl.semaphore_signal(barrier, inc=1, device_id=(x, y), device_id_type=MESH)

    for d in range(1, nx):
        greet(lax.rem(gx + d, nx), gy)
    for d in range(1, ny):
        greet(gx, lax.rem(gy + d, ny))

    stokes_loads = [
        pltpu.make_async_copy(stokes_hbm.at[x], stokes.at[x], stokes_sem.at[x]) for x in range(rows_x)
    ]
    for load in stokes_loads:
        load.start()

    partial[pl.ds(0, rows_y), :] = jnp.zeros((rows_y, lanes), F32)
    below = partial.shape[0] - (nx * rows_x + 1) * rows_y
    partial[pl.ds((nx * rows_x + 1) * rows_y, below), :] = jnp.zeros((below, lanes), F32)

    def no_edge(side):
        edge_in[side] = jnp.zeros_like(edge_in[side])

    pl.when(gy == 0)(functools.partial(no_edge, 0))
    pl.when(gy == ny - 1)(functools.partial(no_edge, 1))

    loads[1].wait()
    loads[2].wait()
    count = jnp.sum(
        jnp.where(iota((peers, peers), 0) == iota((peers, peers), 1), jnp.broadcast_to(counts[...], (peers, peers)), 0),
        axis=1, keepdims=True,
    )
    placed[:, :slots] = jnp.where(iota((peers, slots), 1) < count, elem[...], -1).astype(F32)
    per = lanes // half
    groups = peers // per
    own_groups = groups // nx
    rows = [jnp.zeros((groups, lanes), F32), jnp.zeros((groups, lanes), F32)]
    for j in range(per):
        part = placed[pl.ds(j, groups, stride=per), :][:, :slots].astype(BF16)
        for side in range(2):
            to = iota((slots, lanes), 0) - side * half
            place = (to >= 0) & (to < half) & (iota((slots, lanes), 1) == to + j * half)
            rows[side] = rows[side] + jnp.dot(
                part, jnp.where(place, 1.0, 0.0).astype(BF16), preferred_element_type=F32
            )
    table_out[...] = jnp.zeros_like(table_out)
    for i in range(nx):
        for side in range(2):
            table_out[i, side * own_groups : (side + 1) * own_groups, :] = rows[side][
                i * own_groups : (i + 1) * own_groups, :
            ]
    table_in[gx] = table_out[gx]

    loads[0].wait()
    zeros = jnp.zeros_like(obs[...])
    weights = jnp.concatenate(
        [jnp.concatenate([obs[...], zeros], axis=1), jnp.concatenate([zeros, obs[...]], axis=1)], axis=0
    )

    def project(c):
        misfit_loads[c].wait()
        first = order[c] * ny
        lo = misfit[pl.ds(first, ny), :half, :].reshape(ny * half, width)
        hi = misfit[pl.ds(first, ny), half:, :].reshape(ny * half, width)
        both = lax.dot_general(
            jnp.concatenate([lo, hi], axis=1), weights, (((1,), (1,)), ((), ())), preferred_element_type=F32
        )
        outgoing[order[c]] = both.astype(BF16).reshape(ny, half, lanes)

    project(0)

    loads[3].wait()
    wide[:, :rows_y] = fric[...]
    faces = [("t", 1, -1, 0), ("b", 0, 1, 0), ("l", 3, 0, -1), ("r", 2, 0, 1)]
    fric_copies = []
    for side, slot, dx, dy in faces:
        fric_copies.append(
            (
                side,
                pltpu.make_async_remote_copy(
                    src_ref=wide, dst_ref=near.at[slot], send_sem=fric_send.at[slot], recv_sem=fric_recv.at[slot],
                    device_id=(gx + dx, gy + dy), device_id_type=MESH,
                ),
            )
        )
    pl.semaphore_wait(barrier, nx + ny - 2)
    for d in range(1, nx):
        pl.semaphore_signal(vouch, inc=1, device_id=(lax.rem(gx + d, nx), gy), device_id_type=MESH)
    for d in range(1, nx):
        other = lax.rem(gx + d, nx)
        pltpu.make_async_remote_copy(
            src_ref=table_out.at[other], dst_ref=table_in.at[gx], send_sem=table_send, recv_sem=table_recv,
            device_id=(other, gy), device_id_type=MESH,
        ).start()

    for c in range(nx):
        if c > 0:
            project(c)

        def send(d, carry, c=c):
            peer = lax.rem(gy + d, ny)
            pltpu.make_async_remote_copy(
                src_ref=outgoing.at[order[c], peer], dst_ref=arrived.at[order[c], gy],
                send_sem=send_sem, recv_sem=recv_sem.at[c], device_id=(gx, peer), device_id_type=MESH,
            ).start()
            return carry

        lax.fori_loop(1, ny, send, 0)

    for side, copy in fric_copies:
        pl.when(has[side])(copy.start)

    for c in range(nx):
        arrived[order[c], gy] = outgoing[order[c], gy]

    def pack(first, last):
        for x in range(first, last):
            stokes_loads[x].wait()
            packed[x] = jnp.concatenate([stokes[x, : rows_y // 2], stokes[x, rows_y // 2 :]], axis=-1)

    pack(0, 2)

    table_all = table_in.at[pl.ds(0, nx - 1)]
    pltpu.make_async_copy(table_all, table_all, table_recv).wait()
    which = iota((elements, lanes), 0).astype(F32)
    for i in range(nx):
        for side in range(2):
            for g in range(own_groups):
                row = jnp.broadcast_to(table_in[i, side * own_groups + g : side * own_groups + g + 1, :], (elements, lanes))
                onehot[i, side * elements : (side + 1) * elements, g * lanes : (g + 1) * lanes] = jnp.where(
                    which == row, 1.0, 0.0
                ).astype(BF16)

    pl.semaphore_wait(vouch, nx - 1)
    left_lanes = iota((elements, lanes), 1) < blk
    span = reach * rows_y // 2
    window_lanes = iota((span, lanes), 1) < blk

    def pass_on(to):
        first = to * elements
        one = partial[pl.ds(first, span), :]
        two = partial[pl.ds(first + span, span), :]
        window = jnp.where(window_lanes, one, two).astype(BF16)

        def keep():
            window_in[gx] = window

        def give():
            window_out[to] = window
            pltpu.make_async_remote_copy(
                src_ref=window_out.at[to], dst_ref=window_in.at[gx], send_sem=window_send, recv_sem=window_recv,
                device_id=(to, gy), device_id_type=MESH,
            ).start()

        pl.when(to == gx)(keep)
        pl.when(to != gx)(give)
        for side, there, dy, column in ((0, "r", 1, rows_y - 1), (1, "l", -1, 0)):
            edge_out[side, to] = partial[pl.ds(first + column, 16, stride=rows_y), :].astype(BF16)

            def give_edge(side=side, dy=dy):
                pltpu.make_async_remote_copy(
                    src_ref=edge_out.at[side, to], dst_ref=edge_in.at[side, gx],
                    send_sem=edge_send.at[side], recv_sem=edge_recv.at[side],
                    device_id=(to, gy + dy), device_id_type=MESH,
                ).start()

            pl.when(has[there])(give_edge)

    for c in range(nx):
        now = order[c]
        landed = arrived.at[now, pl.ds(0, ny - 1)]
        pltpu.make_async_copy(landed, landed, recv_sem.at[c]).wait()
        sums = jnp.dot(
            onehot[now], arrived[now].reshape(ny * half, lanes), preferred_element_type=F32
        )
        mixed = jnp.where(left_lanes, sums[:elements], sums[elements:])
        partial[pl.ds(rows_y + now * elements, elements), :] = mixed + pltpu.roll(mixed, blk, axis=1)
        if c > 0:
            pass_on(order[c - 1])
    pass_on(order[nx - 1])

    loads[4].wait()
    eye = jnp.where(iota((rows_y, rows_y), 0) == iota((rows_y, rows_y), 1), 1.0, 0.0)
    tags = pat[...].astype(F32).reshape(offsets * rows_x, rows_y)
    tags = jnp.broadcast_to(tags[:, None, :], (offsets * rows_x, rows_y, rows_y)) * eye[None]
    spread = jnp.dot(
        tags.reshape(offsets * elements, rows_y).astype(BF16), jnp.ones((rows_y, lanes), BF16),
        preferred_element_type=F32,
    )
    present[...] = spread.astype(BF16).reshape(offsets, rows_x, rows_y, lanes)
    pack(2, rows_x)

    window_all = window_in.at[pl.ds(0, nx - 1)]
    pltpu.make_async_copy(window_all, window_all, window_recv).wait()
    total = window_in[0].astype(F32)
    for i in range(1, nx):
        total = total + window_in[i].astype(F32)
    turned = pltpu.roll(total, blk, axis=1)
    for part, rows_of in enumerate((jnp.where(window_lanes, total, turned), jnp.where(window_lanes, turned, total))):
        for r in range(reach // 2):
            cells[part * (reach // 2) + r, 8 : 8 + rows_y] = rows_of[r * rows_y : (r + 1) * rows_y]
    for side, there, at in ((0, "l", 7), (1, "r", 8 + rows_y)):
        edges = pltpu.make_async_copy(edge_in.at[side], edge_in.at[side], edge_recv.at[side])
        pl.when(has[there])(edges.wait)
        edge = edge_in[side, 0].astype(F32)
        for i in range(1, nx):
            edge = edge + edge_in[side, i].astype(F32)
        for r in range(reach):
            cells[r, at : at + 1, :] = edge[r : r + 1, :]
    for q in (-1, 0, 1):
        for r in range(reach):
            shifted[q + 1, r] = cells[r, 8 - q : 8 - q + rows_y, :].astype(BF16)

    lane_block = iota((rows_y, lanes), 1) // blk
    row_of = iota((rows_y, lanes), 0)
    masks = [
        jnp.where(lax.rem(row_of, rows_y // 2) == 2 * c + lane_block, 1.0, 0.0).astype(BF16)
        for c in range(rows_y // 4)
    ]

    def row(x, carry):
        total = jnp.zeros((rows_y, lanes), F32)
        for k in range(9):
            p, q = k // 3 - 1, k % 3 - 1
            source = shifted[q + 1, 1 + x - p] * present[k, x]
            left = jnp.concatenate([source * mask for mask in masks], axis=1)
            right = packed[x, :, k].reshape(rows_y // 2 * blk, lanes)
            total = total + jnp.dot(left, right, preferred_element_type=F32)
        adj_ref[x] = jnp.where(row_of < rows_y // 2, total, pltpu.roll(total, blk, axis=1))[:, :blk]
        return carry

    lax.fori_loop(0, rows_x, row, 0, unroll=8)

    loads[5].wait()
    for side, copy in fric_copies:
        pl.when(has[side])(copy.wait_send)
    for side, slot, dx, dy in faces:
        back = [c for c in fric_copies if c[0] == {"t": "b", "b": "t", "l": "r", "r": "l"}[side]][0][1]
        pl.when(has[side])(back.wait_recv)
    level = wide[...]
    row_id, lane_id = iota(level.shape, 0), iota(level.shape, 1)
    above = jnp.where(row_id == 0, pltpu.roll(near[0], 1, axis=0), pltpu.roll(level, 1, axis=0))
    below = jnp.where(
        row_id == rows_x - 1, pltpu.roll(near[1], rows_x - 1, axis=0), pltpu.roll(level, rows_x - 1, axis=0)
    )
    width_f = level.shape[1]
    before = jnp.where(
        lane_id == 0, pltpu.roll(near[2], width_f - rows_y + 1, axis=1), pltpu.roll(level, 1, axis=1)
    )
    after = jnp.where(
        lane_id == rows_y - 1, pltpu.roll(near[3], rows_y - 1, axis=1), pltpu.roll(level, width_f - 1, axis=1)
    )
    smooth = 0.5 * (4.0 * level - (above + below + before + after))
    work = []
    for x in range(rows_x):
        column = jnp.sum(vel[x].astype(F32) * adj_ref[x], axis=1, keepdims=True)
        work.append(jnp.sum(jnp.broadcast_to(column, (rows_y, rows_y)) * eye, axis=0, keepdims=True))
    work = jnp.concatenate(work, axis=0)
    grad_ref[...] = jnp.exp(fric[...]) * work + smooth[:, :rows_y]

    sent = outgoing.at[:, pl.ds(0, ny - 1)]
    pltpu.make_async_copy(sent, sent, send_sem).wait()
    table_all = table_out.at[pl.ds(0, nx - 1)]
    pltpu.make_async_copy(table_all, table_all, table_send).wait()
    window_all = window_out.at[pl.ds(0, nx - 1)]
    pltpu.make_async_copy(window_all, window_all, window_send).wait()
    for side, there in ((0, "r"), (1, "l")):
        edges = pltpu.make_async_copy(edge_out.at[side], edge_out.at[side], edge_send.at[side])
        pl.when(has[there])(edges.wait)


def hand_on(adj_in, grad_in, adj_out, grad_out, sem):
    copies = [
        pltpu.make_async_copy(adj_in, adj_out, sem.at[0]), pltpu.make_async_copy(grad_in, grad_out, sem.at[1])
    ]
    for copy in copies:
        copy.start()
    for copy in copies:
        copy.wait()


def per_device(
    nx, ny, misfit, block_counts, slot_element, observe, stokes_blocks, pattern, velocity, log_friction
):
    _, peers, slots, width = misfit.shape
    rows_x, rows_y, offsets, blk, _ = stokes_blocks.shape
    elements = rows_x * rows_y
    lanes = 2 * blk
    half = slots // 2
    args = (
        misfit[0], block_counts, slot_element[0], observe.T, stokes_blocks,
        pattern.transpose(2, 0, 1), velocity, log_friction,
    )
    table = -(-2 * ny * half // (8 * lanes)) * 8
    vm, dma = pltpu.VMEM, pltpu.SemaphoreType.DMA
    made = pl.pallas_call(
        functools.partial(kernel, nx, ny),
        out_shape=(pltpu.VMEM((rows_x, rows_y, blk), F32), pltpu.VMEM((rows_x, rows_y), F32)),
        in_specs=[pl.BlockSpec(memory_space=pltpu.HBM)] * len(args),
        out_specs=(pl.BlockSpec(memory_space=pltpu.VMEM),) * 2,
        scratch_shapes=[vm(a.shape, a.dtype) for a in args]
        + [
            vm((nx, ny, half, lanes), BF16),
            vm((nx, ny, half, lanes), BF16),
            vm((peers, 128), F32),
            vm((nx, table, lanes), F32),
            vm((nx, table, lanes), F32),
            vm((nx, 2 * elements, ny * half), BF16),
            vm((offsets, rows_x, rows_y, lanes), BF16),
            vm(((nx * rows_x + 8 + 2) * rows_y, lanes), F32),
            vm((nx, (rows_x + 2) * rows_y // 2, lanes), BF16),
            vm((nx, (rows_x + 2) * rows_y // 2, lanes), BF16),
            vm((2, nx, 16, lanes), BF16),
            vm((2, nx, 16, lanes), BF16),
            vm((rows_x + 2, rows_y + 16, lanes), F32),
            vm((3, rows_x + 2, rows_y, lanes), BF16),
            vm((rows_x, 128), F32),
            vm((4, rows_x, 128), F32),
            dma((nx,)),
            dma((6,)),
            dma((rows_x,)),
            dma,
            dma((nx,)),
            dma,
            dma,
            dma((4,)),
            dma((4,)),
            dma,
            dma,
            dma((2,)),
            dma((2,)),
            pltpu.SemaphoreType.REGULAR,
            vm((rows_x, rows_y // 2, offsets, blk, lanes), BF16),
        ],
        compiler_params=pltpu.CompilerParams(
            collective_id=0, has_side_effects=True, vmem_limit_bytes=60 * 1024 * 1024
        ),
    )(*args)
    return pl.pallas_call(
        hand_on,
        out_shape=tuple(jax.ShapeDtypeStruct(a.shape, a.dtype) for a in made),
        in_specs=[pl.BlockSpec(memory_space=pltpu.VMEM)] * 2,
        out_specs=(pl.BlockSpec(memory_space=pltpu.HBM),) * 2,
        scratch_shapes=[pltpu.SemaphoreType.DMA((2,))],
        compiler_params=pltpu.CompilerParams(vmem_limit_bytes=1024 * 1024),
    )(*made)


def solution(mesh):
    in_specs = (
        P(("gx", "gy"), None, None, None),
        P(("gx", "gy"), None),
        P(("gx", "gy"), None, None),
        P(),
        P("gx", "gy", None, None, None),
        P("gx", "gy", None),
        P("gx", "gy", None),
        P("gx", "gy"),
    )
    out_specs = (P("gx", "gy", None), P("gx", "gy"))
    return jax.shard_map(
        functools.partial(per_device, mesh.shape["gx"], mesh.shape["gy"]),
        mesh=mesh, in_specs=in_specs, out_specs=out_specs, check_vma=False,
    )
```

time: 19.1 us -> 17.2 us (0.901)
  Pallas kernels: 18.3 us -> 16.4 us
    pallas_call x1, Pallas kernels: 17.6 us -> 15.7 us  [per_device(): pl.pallas_call(functools.partial(kernel, nx, ny), out_shape=(pltpu.VMEM((...]
where the time goes in v2:
time: 17.2 us; the launch traced here: 17 us
  Pallas kernels  16.4 us (95%)
  between operations  0.64 us (4%)
    pallas_call x1, Pallas kernels, per_device(): pl.pallas_call(functools.partial(kernel, nx, ny), out_shape=(pltpu.VMEM((...  15.7 us
    pallas_call x1, Pallas kernels, per_device(): pl.pallas_call(hand_on, out_shape=tuple((jax.ShapeDtypeStruct(a.shape, a....  0.65 us

profile of v2, /device:TPU:1, one launch (start us, length us, event | category | flops | bytes accessed | tf_op | source)
XLA Modules:
  0.0 17.0 jit_solution(10080492460634540371)
XLA Ops:
  0.6 15.7 %shard_map.95 = (f32[8,16,64]{2,1,0:T(8,128)S(1)}, f32[8,16]{1,0:T(8,128)S(1)}) custom-call(bf16[32,64,128]{2,1,0:T(8,128)(2,1)} %bitcast.4, s32[1,32]{1,0:T(1,128)} %counts_hbm.1, s32[32,64]{1,0:T(8,128)} %bitcast.6, bf16[64,128]{1,0:T(8,128)(2,1)} %bitcast.7, bf16[8,16,9,64,64]{4,3,2,1,0:T(8,128)(2,1)} %stokes_hbm.1, s32[9,8,16]{2,1,0:T(8,128)} %bitcast.5, ...), custom_call_target="tpu_custom_call" | custom-call | tf_op jit(solution)/shard_map/pallas_call | solution.py:354
  16.4 0.7 %shard_map.96 = (f32[8,16,64]{2,1,0:T(8,128)}, f32[8,16]{1,0:T(8,128)}) custom-call(f32[8,16,64]{2,1,0:T(8,128)S(1)} %get-tuple-element.4.adj_in, f32[8,16]{1,0:T(8,128)S(1)} %get-tuple-element.5.grad_in), custom_call_target="tpu_custom_call" | custom-call | tf_op jit(solution)/shard_map/pallas_call | solution.py:397

commit v3 on v2

--- a/solution.py
+++ b/solution.py
@@ -35,7 +35,7 @@
     gx, gy = lax.axis_index("gx"), lax.axis_index("gy")
     has = {"t": gx > 0, "b": gx < nx - 1, "l": gy > 0, "r": gy < ny - 1}
 
-    high = (2 * gx) // nx
+    high = (gx + nx - 1) // nx
     order = [(1 - high) * (nx - 1 - c) + high * c for c in range(nx)]
 
     misfit_loads = [
@@ -176,7 +176,7 @@
             stokes_loads[x].wait()
             packed[x] = jnp.concatenate([stokes[x, : rows_y // 2], stokes[x, rows_y // 2 :]], axis=-1)
 
-    pack(0, 2)
+    pack(0, 5)
 
     table_all = table_in.at[pl.ds(0, nx - 1)]
     pltpu.make_async_copy(table_all, table_all, table_recv).wait()
@@ -246,7 +246,7 @@
         preferred_element_type=F32,
     )
     present[...] = spread.astype(BF16).reshape(offsets, rows_x, rows_y, lanes)
-    pack(2, rows_x)
+    pack(5, rows_x)
 
     window_all = window_in.at[pl.ds(0, nx - 1)]
     pltpu.make_async_copy(window_all, window_all, window_recv).wait()
@@ -365,7 +365,7 @@
             vm((nx, table, lanes), F32),
             vm((nx, 2 * elements, ny * half), BF16),
             vm((offsets, rows_x, rows_y, lanes), BF16),
-            vm(((nx * rows_x + 8 + 2) * rows_y, lanes), F32),
+            vm(((nx * rows_x + 8 * 4) * rows_y, lanes), F32),
             vm((nx, (rows_x + 2) * rows_y // 2, lanes), BF16),
             vm((nx, (rows_x + 2) * rows_y // 2, lanes), BF16),
             vm((2, nx, 16, lanes), BF16),

time: 17.2 us -> 17.2 us (level)
  no operation moved by 1% of the time
where the time goes in v3:
time: 17.2 us; the launch traced here: 17 us
  Pallas kernels  16.4 us (95%)
  between operations  0.64 us (4%)
    pallas_call x1, Pallas kernels, per_device(): pl.pallas_call(functools.partial(kernel, nx, ny), out_shape=(pltpu.VMEM((...  15.7 us
    pallas_call x1, Pallas kernels, per_device(): pl.pallas_call(hand_on, out_shape=tuple((jax.ShapeDtypeStruct(a.shape, a....  0.65 us

profile of v3, /device:TPU:1, one launch (start us, length us, event | category | flops | bytes accessed | tf_op | source)
XLA Modules:
  0.0 17.0 jit_solution(6152471178514588918)
XLA Ops:
  0.6 15.7 %shard_map.95 = (f32[8,16,64]{2,1,0:T(8,128)S(1)}, f32[8,16]{1,0:T(8,128)S(1)}) custom-call(bf16[32,64,128]{2,1,0:T(8,128)(2,1)} %bitcast.4, s32[1,32]{1,0:T(1,128)} %counts_hbm.1, s32[32,64]{1,0:T(8,128)} %bitcast.6, bf16[64,128]{1,0:T(8,128)(2,1)} %bitcast.7, bf16[8,16,9,64,64]{4,3,2,1,0:T(8,128)(2,1)} %stokes_hbm.1, s32[9,8,16]{2,1,0:T(8,128)} %bitcast.5, ...), custom_call_target="tpu_custom_call" | custom-call | tf_op jit(solution)/shard_map/pallas_call | solution.py:354
  16.4 0.7 %shard_map.96 = (f32[8,16,64]{2,1,0:T(8,128)}, f32[8,16]{1,0:T(8,128)}) custom-call(f32[8,16,64]{2,1,0:T(8,128)S(1)} %get-tuple-element.4.adj_in, f32[8,16]{1,0:T(8,128)S(1)} %get-tuple-element.5.grad_in), custom_call_target="tpu_custom_call" | custom-call | tf_op jit(solution)/shard_map/pallas_call | solution.py:397

commit v4 on v3

--- a/solution.py
+++ b/solution.py
@@ -50,7 +50,7 @@
             ((obs_hbm, obs), (elem_hbm, elem), (counts_hbm, counts), (fric_hbm, fric), (pat_hbm, pat), (vel_hbm, vel))
         )
     ]
-    for load in loads[:3] + misfit_loads + loads[3:]:
+    for load in loads[:1] + misfit_loads[:1] + loads[1:3] + misfit_loads[1:] + loads[3:]:
         load.start()
 
     for ref in (wide, near):

time: 17.2 us -> 17.2 us (level)
  no operation moved by 1% of the time
where the time goes in v4:
time: 17.2 us; the launch traced here: 17 us
  Pallas kernels  16.4 us (95%)
  between operations  0.64 us (4%)
    pallas_call x1, Pallas kernels, per_device(): pl.pallas_call(functools.partial(kernel, nx, ny), out_shape=(pltpu.VMEM((...  15.7 us
    pallas_call x1, Pallas kernels, per_device(): pl.pallas_call(hand_on, out_shape=tuple((jax.ShapeDtypeStruct(a.shape, a....  0.65 us

profile of v4, /device:TPU:1, one launch (start us, length us, event | category | flops | bytes accessed | tf_op | source)
XLA Modules:
  0.0 17.0 jit_solution(10607920015002759508)
XLA Ops:
  0.6 15.7 %shard_map.95 = (f32[8,16,64]{2,1,0:T(8,128)S(1)}, f32[8,16]{1,0:T(8,128)S(1)}) custom-call(bf16[32,64,128]{2,1,0:T(8,128)(2,1)} %bitcast.4, s32[1,32]{1,0:T(1,128)} %counts_hbm.1, s32[32,64]{1,0:T(8,128)} %bitcast.6, bf16[64,128]{1,0:T(8,128)(2,1)} %bitcast.7, bf16[8,16,9,64,64]{4,3,2,1,0:T(8,128)(2,1)} %stokes_hbm.1, s32[9,8,16]{2,1,0:T(8,128)} %bitcast.5, ...), custom_call_target="tpu_custom_call" | custom-call | tf_op jit(solution)/shard_map/pallas_call | solution.py:354
  16.4 0.7 %shard_map.96 = (f32[8,16,64]{2,1,0:T(8,128)}, f32[8,16]{1,0:T(8,128)}) custom-call(f32[8,16,64]{2,1,0:T(8,128)S(1)} %get-tuple-element.4.adj_in, f32[8,16]{1,0:T(8,128)S(1)} %get-tuple-element.5.grad_in), custom_call_target="tpu_custom_call" | custom-call | tf_op jit(solution)/shard_map/pallas_call | solution.py:397

commit v5 on v4

--- a/solution.py
+++ b/solution.py
@@ -211,7 +211,8 @@
             ).start()
 
         pl.when(to == gx)(keep)
-        pl.when(to != gx)(give)
+        away = to != gx
+        pl.when(jnp.logical_and(away, gy == 0))(give)
         for side, there, dy, column in ((0, "r", 1, rows_y - 1), (1, "l", -1, 0)):
             edge_out[side, to] = partial[pl.ds(first + column, 16, stride=rows_y), :].astype(BF16)
 
@@ -223,6 +224,7 @@
                 ).start()
 
             pl.when(has[there])(give_edge)
+        pl.when(jnp.logical_and(away, gy > 0))(give)
 
     for c in range(nx):
         now = order[c]

time: 17.2 us -> 17 us (0.988)
  the two profiles are of different devices: /device:TPU:1 before, /device:TPU:0 now
where the time goes in v5:
time: 17 us; the launch traced here: 16.8 us
  Pallas kernels  16.2 us (95%)
  between operations  0.64 us (4%)
    pallas_call x1, Pallas kernels, per_device(): pl.pallas_call(functools.partial(kernel, nx, ny), out_shape=(pltpu.VMEM((...  15.5 us
    pallas_call x1, Pallas kernels, per_device(): pl.pallas_call(hand_on, out_shape=tuple((jax.ShapeDtypeStruct(a.shape, a....  0.65 us

profile of v5, /device:TPU:0, one launch (start us, length us, event | category | flops | bytes accessed | tf_op | source)
XLA Modules:
  0.0 16.8 jit_solution(4503328400044257548)
XLA Ops:
  0.6 15.5 %shard_map.95 = (f32[8,16,64]{2,1,0:T(8,128)S(1)}, f32[8,16]{1,0:T(8,128)S(1)}) custom-call(bf16[32,64,128]{2,1,0:T(8,128)(2,1)} %bitcast.4, s32[1,32]{1,0:T(1,128)} %counts_hbm.1, s32[32,64]{1,0:T(8,128)} %bitcast.6, bf16[64,128]{1,0:T(8,128)(2,1)} %bitcast.7, bf16[8,16,9,64,64]{4,3,2,1,0:T(8,128)(2,1)} %stokes_hbm.1, s32[9,8,16]{2,1,0:T(8,128)} %bitcast.5, ...), custom_call_target="tpu_custom_call" | custom-call | tf_op jit(solution)/shard_map/pallas_call | solution.py:356
  16.2 0.7 %shard_map.96 = (f32[8,16,64]{2,1,0:T(8,128)}, f32[8,16]{1,0:T(8,128)}) custom-call(f32[8,16,64]{2,1,0:T(8,128)S(1)} %get-tuple-element.4.adj_in, f32[8,16]{1,0:T(8,128)S(1)} %get-tuple-element.5.grad_in), custom_call_target="tpu_custom_call" | custom-call | tf_op jit(solution)/shard_map/pallas_call | solution.py:399
